TPU v7x, 128 devices: a whole 4x4x4 slice. The times are simulated.
128 devices in a mesh: sec: 2 (over core), lon: 32 (over z_lo, y, x), lat: 2 (over z_hi).
Axes of the slice: x: 4, y: 4, z: 4 (z_hi: 2, z_lo: 2; z = z_hi * 2 + z_lo), core: 2. Of those that a mesh axis runs over, the one named last changes fastest.
Arguments:
- atm_state: bfloat16 [4096, 256, 256], P(('sec', 'lon', 'lat')), may hold values from -6 to 6
- cost_class: int32 [4096], P(('sec', 'lon', 'lat')), may hold values from 1 to 8, as said below
- w_in: bfloat16 [384, 256], replicated, may hold values from -0.375 to 0.375
- w_out: bfloat16 [256, 384], replicated, may hold values from -0.3125 to 0.3125
- w_flux: bfloat16 [4, 256], replicated, may hold values from -0.375 to 0.375
- feeding_block_index: int32 [16, 64, 4], P('lat', ('sec', 'lon')), may hold values from 0 to 4095, as said below
- pairwise_remap_weight: bfloat16 [16, 64, 4, 256, 256], P('lat', ('sec', 'lon')), may hold values from -0.1875 to 0.1875
- ocean_tracers: float32 [2, 40, 16, 16384], P(None, None, 'lat', ('sec', 'lon')), may hold values from -6 to 6
- land_sea: int32 [16, 16384], P('lat', ('sec', 'lon')), may hold values 0 or 1
Outputs:
- column_state_next: bfloat16 [4096, 256, 256], P(('sec', 'lon', 'lat'))
- tracer_fields_next: float32 [2, 40, 16, 16384], P(None, None, 'lat', ('sec', 'lon'))
- atmos_surface_temp: float32 [4096, 256], P(('sec', 'lon', 'lat'))
Inputs may be any that keep to these rules, and one draw needn't show every extreme that they name: `cost_class`: all 32 blocks of one device share one class; among devices that differ only in their lon index, 16 hold class 1, 8 class 2 and 8 class 8. `feeding_block_index`: entry [r, c, k] is ((s * 32 + q) * 2 + t) * 32 + l with t = r // 8, s = c // 32, l = c % 32 and some q below 32; every atmosphere block is named exactly once.
All inputs are finite; a program needn't handle non-finite values. No bound on the sum of `land_sea` on one device may be relied on, other than what follows from the above.
Results may differ from a plain program's by a relative error of at most 0.013.
Values may be sent and summed in bfloat16 or wider, within the bound.
A program may use at most 64 MiB of HBM per device.

v0:
```python
import jax
import jax.numpy as jnp
from jax import lax
from jax.sharding import PartitionSpec as P


def with_halo(block, sides, width):
    for axis, dim in sides:
        count = lax.axis_size(axis)
        forward = [(i, i + 1) for i in range(count - 1)]
        backward = [(target, source) for source, target in forward]
        low = lax.ppermute(
            lax.slice_in_dim(block, block.shape[dim] - width, None, axis=dim), axis, forward
        )
        high = lax.ppermute(lax.slice_in_dim(block, 0, width, axis=dim), axis, backward)
        block = jnp.concatenate([low, block, high], axis=dim)
    return block


def column_update(current, w_in, w_out):
    hidden = jnp.einsum("hf,bfc->bhc", w_in, current, preferred_element_type=jnp.float32)
    hidden = jax.nn.silu(hidden).astype(jnp.bfloat16)
    change = jnp.einsum("fh,bhc->bfc", w_out, hidden, preferred_element_type=jnp.float32)
    return (current.astype(jnp.float32) + 0.5 * change).astype(jnp.bfloat16)


def ocean_update(padded, padded_mask, tracers, mask, forcing):
    levels = tracers.shape[1]
    row_count = tracers.shape[2]
    col_count = tracers.shape[3]
    spread = jnp.zeros_like(tracers)
    for row_shift, col_shift in ((0, 1), (2, 1), (1, 0), (1, 2)):
        neighbour = padded[
            :, :, row_shift : row_shift + row_count, col_shift : col_shift + col_count
        ]
        near_mask = padded_mask[
            row_shift : row_shift + row_count, col_shift : col_shift + col_count
        ]
        spread = spread + near_mask * (neighbour - tracers)
    wind_stress = forcing[3]
    top_mixing = 0.1 + 0.3 * wind_stress * wind_stress / (1.0 + wind_stress * wind_stress)
    mixing = jnp.concatenate(
        [top_mixing[None], jnp.full((levels - 2, row_count, col_count), 0.1, jnp.float32)], 0
    )
    vertical_flux = mixing[None] * (tracers[:, 1:] - tracers[:, :-1])
    zero_layer = jnp.zeros((2, 1, row_count, col_count), jnp.float32)
    vertical = jnp.concatenate([vertical_flux, zero_layer], 1) - jnp.concatenate(
        [zero_layer, vertical_flux], 1
    )
    depth_index = jnp.arange(levels, dtype=jnp.float32)
    fraction = jnp.exp(-depth_index / 8.0) - jnp.exp(-(depth_index + 1.0) / 8.0)
    surface = (depth_index == 0.0).astype(jnp.float32)
    heating = 0.5 * (
        forcing[1][None] * fraction[:, None, None] + forcing[0][None] * surface[:, None, None]
    )
    freshening = 0.3 * forcing[2][None] * surface[:, None, None]
    source = jnp.stack([heating, freshening], 0)
    return tracers + mask * (0.2 * spread + vertical + source)


def per_device(
    atm_state,
    cost_class,
    w_in,
    w_out,
    w_flux,
    feeding_block_index,
    pairwise_remap_weight,
    ocean_tracers,
    land_sea,
):
    lon_count = lax.axis_size("lon")
    lat_count = lax.axis_size("lat")
    blocks = atm_state.shape[0]
    per_peer = blocks // lon_count

    def substep(counter, current):
        renewed = column_update(current, w_in, w_out)
        return jnp.where((cost_class > counter)[:, None, None], renewed, current)

    column_state_next = lax.fori_loop(jnp.int32(0), jnp.max(cost_class), substep, atm_state)
    fluxes = jnp.einsum(
        "gf,bfc->bgc", w_flux, column_state_next, preferred_element_type=jnp.float32
    ).astype(jnp.bfloat16)
    row_count = feeding_block_index.shape[0]
    remap_count = feeding_block_index.shape[2]
    index_flat = feeding_block_index.reshape(-1)
    source_device = index_flat // blocks
    source_slot = index_flat % blocks
    source_lon = source_device // lat_count % lon_count
    exchange_position = source_lon * per_peer + source_slot % per_peer
    arrived_flux = lax.all_gather(fluxes, "lon", axis=0, tiled=True)
    position = source_lon * blocks + source_slot
    block_width = fluxes.shape[2]
    picked = arrived_flux[position].reshape(row_count, remap_count, 4, block_width)
    weight_on_device = pairwise_remap_weight[:, 0]
    ocean_flux = jnp.einsum(
        "rkgx,rkxy->gry", picked, weight_on_device, preferred_element_type=jnp.float32
    )
    levels = ocean_tracers.shape[1]
    col_count = ocean_tracers.shape[3]
    mask = land_sea.astype(jnp.float32)
    stacked = jnp.concatenate(
        [ocean_tracers.reshape(2 * levels, row_count, col_count), mask[None]], 0
    )
    padded_all = with_halo(
        stacked.astype(jnp.bfloat16), ((("sec", "lon"), 2), ("lat", 1)), 1
    ).astype(stacked.dtype)
    padded = padded_all[:-1].reshape(2, levels, row_count + 2, col_count + 2)
    padded_mask = padded_all[-1]
    tracer_fields_next = ocean_update(padded, padded_mask, ocean_tracers, mask, ocean_flux)
    surface_temp_shipped = tracer_fields_next[0, 0].astype(jnp.bfloat16)
    weighted_terms = jnp.einsum(
        "flve,fe->flv", weight_on_device, surface_temp_shipped, preferred_element_type=jnp.float32
    )
    weighted_terms_flat = weighted_terms.reshape(row_count * remap_count, block_width)
    inverse_order = jnp.argsort(exchange_position)
    atmos_surface_temp = lax.all_to_all(
        weighted_terms_flat[inverse_order].astype(jnp.bfloat16),
        "lon",
        split_axis=0,
        concat_axis=0,
        tiled=True,
    ).astype(jnp.float32)
    return (column_state_next, tracer_fields_next, atmos_surface_temp)


def solution(mesh):
    return jax.shard_map(
        per_device,
        mesh=mesh,
        in_specs=(
            P(("sec", "lon", "lat"), None, None),
            P(("sec", "lon", "lat")),
            P(),
            P(),
            P(),
            P("lat", ("sec", "lon"), None),
            P("lat", ("sec", "lon"), None, None, None),
            P(None, None, "lat", ("sec", "lon")),
            P("lat", ("sec", "lon")),
        ),
        out_specs=(
            P(("sec", "lon", "lat"), None, None),
            P(None, None, "lat", ("sec", "lon")),
            P(("sec", "lon", "lat"), None),
        ),
        check_vma=False,
    )
```

profile of v0, /device:TPU:0, one launch (start us, length us, event | category | flops | bytes accessed | tf_op | source)
XLA Modules:
  0.0 346.7 jit_solution(12352057217476699272)
XLA Ops:
  7.3 6.6 %copy.31 = bf16[32,256,256]{1,2,0:T(8,128)(2,1)} copy(bf16[32,256,256]{2,1,0:T(8,128)(2,1)} %param.11) | data formatting | bytes 8388608 | tf_op jit(solution)/shard_map/while | solution.py:81
  14.5 17.9 %while.10 = (s32[]{:T(128)}, bf16[32,256,256]{1,2,0:T(8,128)(2,1)}, s32[]{:T(128)}, s32[32]{0:T(128)S(1)}, bf16[384,256]{1,0:T(8,128)(2,1)S(1)}, /*index=5*/bf16[256,384]{1,0:T(8,128)(2,1)S(1)}, s32[]{:T(128)}) while((s32[]{:T(128)}, bf16[32,256,256]{1,2,0:T(8,128)(2,1)}, s32[]{:T(128)}, s32[32]{0:T(128)S(1)}, bf16[384,256]{1,0:T(8,128)(2,1)S(1)}, ...), condition=%wide.region_2.3_spmd, body=%wide.region_1.2_spmd.sunk | while | flops 3247439872 | bytes 17170704 | solution.py:81
  15.1 4.6 %copy.61 = bf16[32,256,256]{1,2,0:T(8,128)(2,1)} copy(bf16[32,256,256]{1,2,0:T(8,128)(2,1)} %get-tuple-element.149) | data formatting | bytes 8388608 | tf_op jit(solution)/shard_map/while
  19.8 11.9 %fusion.69 = bf16[32,256,256]{1,2,0:T(8,128)(2,1)} fusion(bf16[32,256,256]{1,2,0:T(8,128)(2,1)} %copy.61, pred[32]{0:T(512)(128)(4,1)S(1)} %broadcast_compare_fusion.2, bf16[256,384]{1,0:T(8,128)(2,1)S(1)} %get-tuple-element.160, bf16[384,256]{1,0:T(8,128)(2,1)S(1)} %get-tuple-element.159), kind=kOutput, calls=%fused_computation.10.clone.1 | convolution fusion | flops 3247439872 | bytes 8781856 | tf_op jit(solution)/shard_map/while/body/fh,bhc->bfc/dot_general | solution.py:23
  32.4 4.1 %fusion.20 = bf16[32,4,256]{2,1,0:T(4,128)(2,1)} fusion(bf16[32,256,256]{1,2,0:T(8,128)(2,1)} %get-tuple-element.72, bf16[4,256]{1,0:T(4,128)(2,1)S(1)} %copy-done), kind=kOutput, calls=%fused_computation.22 | convolution fusion | flops 16809984 | bytes 4261888 | tf_op jit(solution)/shard_map/gf,bfc->bgc/dot_general | solution.py:82
  36.7 3.5 %collective-permute-start = (bf16[81,8,1]{2,1,0:T(8,128)(2,1)S(1)}, bf16[81,8,1]{2,1,0:T(8,128)(2,1)S(1)}, u32[]{:S(2)}, u32[]{:S(2)}) collective-permute-start(bf16[81,8,1]{2,1,0:T(8,128)(2,1)S(1)} %get-tuple-element.89), channel_id=1, source_target_pairs={{0,2},{2,4},{4,6},{6,8},{8,10},{10,12},{12,14},{14,16},{16,18},{18... | collective-permute-start | bytes 3896 | tf_op jit(solution)/shard_map/ppermute | solution.py:12
  40.2 1.3 collective-permute-start.1
  41.8 1.6 sort.17
  43.5 124.1 %collective-permute-done.1 = bf16[81,8,1]{2,1,0:T(8,128)(2,1)S(1)} collective-permute-done((bf16[81,8,1]{2,1,0:T(8,128)(2,1)S(1)}, bf16[81,8,1]{2,1,0:T(8,128)(2,1)S(1)}, u32[]{:S(2)}, u32[]{:S(2)}) %collective-permute-start.1) | collective-permute-done | bytes 1328 | tf_op jit(solution)/shard_map/ppermute | solution.py:15
  168.2 6.4 %collective-permute-start.2 = (bf16[81,1,258]{2,1,0:T(2,128)(2,1)S(1)}, bf16[81,1,258]{2,1,0:T(2,128)(2,1)S(1)}, u32[]{:S(2)}, u32[]{:S(2)}) collective-permute-start(bf16[81,1,258]{2,1,0:T(2,128)(2,1)S(1)} %get-tuple-element.87), channel_id=1, source_target_pairs={{0,1},{2,3},{4,5},{6,7},{8,9},{10,11},{12,13},{14,15},{16,17},{18,... | collective-permute-start | bytes 125396 | tf_op jit(solution)/shard_map/ppermute | solution.py:12
  174.6 1.3 collective-permute-start.3
  175.9 2.3 collective-permute-done.2
  178.2 5.8 %collective-permute-done.3 = bf16[81,1,258]{2,1,0:T(2,128)(2,1)S(1)} collective-permute-done((bf16[81,1,258]{2,1,0:T(2,128)(2,1)S(1)}, bf16[81,1,258]{2,1,0:T(2,128)(2,1)S(1)}, u32[]{:S(2)}, u32[]{:S(2)}) %collective-permute-start.3) | collective-permute-done | bytes 41828 | tf_op jit(solution)/shard_map/ppermute | solution.py:15
  184.0 1.0 fusion.24
  185.1 127.5 %all-gather.2.cloned.1.call-done = bf16[1024,4,256]{2,1,0:T(4,128)(2,1)} async-done(((bf16[32,4,256]{2,1,0:T(4,128)(2,1)}), bf16[1024,4,256]{2,1,0:T(4,128)(2,1)}) %all-gather.2.cloned.1.call-update) | async-done | bytes 2097168 | tf_op jit(solution)/shard_map/all_gather | solution.py:92
  312.6 2.2 gather_fusion
  314.8 2.9 fusion.21
  318.0 0.7 fusion.31
  318.7 1.4 copy-done.1
  320.1 1.2 fusion.16
  322.5 0.7 reduce
  323.8 7.2 %all-to-all-start = ((bf16[32,2,128]{2,1,0:T(2,128)(2,1)}), bf16[32,2,128]{2,1,0:T(2,128)(2,1)S(1)}, u32[]{:S(2)}, u32[]{:S(2)}) async-start(bf16[32,2,128]{2,1,0:T(2,128)(2,1)} %reshape.296), calls=%async_computation | async-start | bytes 32768 | tf_op jit(solution)/shard_map/all_to_all | solution.py:118
  331.0 6.4 %copy.37 = bf16[32,256,256]{2,1,0:T(8,128)(2,1)} copy(bf16[32,256,256]{1,2,0:T(8,128)(2,1)} %get-tuple-element.72) | data formatting | bytes 8388608
  337.4 1.8 all-to-all-done
  (52 shorter events, 4.7 us)
Async XLA Ops:
  7.2 25.2 %copy-start = (bf16[4,256]{1,0:T(4,128)(2,1)S(1)}, bf16[4,256]{1,0:T(4,128)(2,1)}, u32[]{:S(2)}) copy-start(bf16[4,256]{1,0:T(4,128)(2,1)} %param.15) | copy-start | bytes 6148
  7.2 6.7 %copy-start.8 = (s32[32]{0:T(128)S(1)}, s32[32]{0:T(128)}, u32[]{:S(2)}) copy-start(s32[32]{0:T(128)} %param.12) | copy-start | bytes 388
  7.2 7.3 %copy-start.6 = (bf16[384,256]{1,0:T(8,128)(2,1)S(1)}, bf16[384,256]{1,0:T(8,128)(2,1)}, u32[]{:S(2)}) copy-start(bf16[384,256]{1,0:T(8,128)(2,1)} %param.13) | copy-start | bytes 589828
  7.2 7.3 %copy-start.7 = (bf16[256,384]{1,0:T(8,128)(2,1)S(1)}, bf16[256,384]{1,0:T(8,128)(2,1)}, u32[]{:S(2)}) copy-start(bf16[256,384]{1,0:T(8,128)(2,1)} %param.14) | copy-start | bytes 589828
  7.2 305.4 %all-gather.2.cloned.1.call-start = ((), (), s32[]{:S(2)}) async-start(), calls=%async_computation.1 | async-start | bytes 2162688 | tf_op jit(solution)/shard_map/all_gather | solution.py:92
  32.4 4.1 %copy-start.2 = (f32[2,40,8,256]{3,2,1,0:T(8,128)S(1)}, f32[2,40,8,256]{3,2,1,0:T(8,128)}, u32[]{:S(2)}) copy-start(f32[2,40,8,256]{3,2,1,0:T(8,128)} %param.18) | copy-start | bytes 1966084
  32.4 4.2 %copy-start.4 = (s32[8,256]{1,0:T(8,128)S(1)}, s32[8,256]{1,0:T(8,128)}, u32[]{:S(2)}) copy-start(s32[8,256]{1,0:T(8,128)} %param.19) | copy-start | bytes 24580
  32.4 9.1 %copy-start.5 = (s32[8,1,4]{0,2,1:T(4,128)S(1)}, s32[8,1,4]{0,2,1:T(4,128)}, u32[]{:S(2)}) copy-start(s32[8,1,4]{0,2,1:T(4,128)} %param.16) | copy-start | bytes 388
  36.7 6.8 %collective-permute-start = (bf16[81,8,1]{2,1,0:T(8,128)(2,1)S(1)}, bf16[81,8,1]{2,1,0:T(8,128)(2,1)S(1)}, u32[]{:S(2)}, u32[]{:S(2)}) collective-permute-start(bf16[81,8,1]{2,1,0:T(8,128)(2,1)S(1)} %get-tuple-element.89), channel_id=1, source_target_pairs={{0,2},{2,4},{4,6},{6,8},{8,10},{10,12},{12,14},{14,16},{16,18},{18... | collective-permute-start | bytes 3896 | tf_op jit(solution)/shard_map/ppermute | solution.py:12
  40.2 127.4 %collective-permute-start.1 = (bf16[81,8,1]{2,1,0:T(8,128)(2,1)S(1)}, bf16[81,8,1]{2,1,0:T(8,128)(2,1)S(1)}, u32[]{:S(2)}, u32[]{:S(2)}) collective-permute-start(bf16[81,8,1]{2,1,0:T(8,128)(2,1)S(1)} %get-tuple-element.90), channel_id=1, source_target_pairs={{2,0},{4,2},{6,4},{8,6},{10,8},{12,10},{14,12},{16,14},{18,16},{20... | collective-permute-start | bytes 3896 | tf_op jit(solution)/shard_map/ppermute | solution.py:15
  168.2 10.0 %collective-permute-start.2 = (bf16[81,1,258]{2,1,0:T(2,128)(2,1)S(1)}, bf16[81,1,258]{2,1,0:T(2,128)(2,1)S(1)}, u32[]{:S(2)}, u32[]{:S(2)}) collective-permute-start(bf16[81,1,258]{2,1,0:T(2,128)(2,1)S(1)} %get-tuple-element.87), channel_id=1, source_target_pairs={{0,1},{2,3},{4,5},{6,7},{8,9},{10,11},{12,13},{14,15},{16,17},{18,... | collective-permute-start | bytes 125396 | tf_op jit(solution)/shard_map/ppermute | solution.py:12
  174.6 9.4 %collective-permute-start.3 = (bf16[81,1,258]{2,1,0:T(2,128)(2,1)S(1)}, bf16[81,1,258]{2,1,0:T(2,128)(2,1)S(1)}, u32[]{:S(2)}, u32[]{:S(2)}) collective-permute-start(bf16[81,1,258]{2,1,0:T(2,128)(2,1)S(1)} %get-tuple-element.88), channel_id=1, source_target_pairs={{1,0},{3,2},{5,4},{7,6},{9,8},{11,10},{13,12},{15,14},{17,16},{19,... | collective-permute-start | bytes 125396 | tf_op jit(solution)/shard_map/ppermute | solution.py:15
  317.7 2.4 copy-start.1
  318.7 2.6 copy-start.3
  323.8 15.4 %all-to-all-start = ((bf16[32,2,128]{2,1,0:T(2,128)(2,1)}), bf16[32,2,128]{2,1,0:T(2,128)(2,1)S(1)}, u32[]{:S(2)}, u32[]{:S(2)}) async-start(bf16[32,2,128]{2,1,0:T(2,128)(2,1)} %reshape.296), calls=%async_computation | async-start | bytes 32768 | tf_op jit(solution)/shard_map/all_to_all | solution.py:118
Sparse Core Ops, SparseCore 0:
  36.6 275.9 all-gather.1
where the time goes:
time: 348 us; the launch traced here: 347 us
  waiting for transfers between devices  261 us (75%)
  local copies, waits for them, and re-layouts  24.1 us (7%)
  matrix products  20 us (6%)
  starting transfers between devices  19.7 us (6%)
  between operations  14.3 us (4%)
  other arithmetic  5.76 us (2%)
    ppermute x2, waiting for transfers between devices, with_halo(): lax.ppermute(lax.slice_in_dim(block, 0, width, axis=dim), axis, backward)  130 us
    all_gather x1, waiting for transfers between devices, per_device(): arrived_flux = lax.all_gather(fluxes, 'lon', axis=0, tiled=True)  127 us
    dot_general x1, matrix products, column_update(): jnp.einsum('fh,bhc->bfc', w_out, hidden, preferred_element_type=jnp.float32)  11.9 us
    ppermute x2, starting transfers between devices, with_halo(): lax.ppermute(lax.slice_in_dim(block, block.shape[dim] - width, None, axis...  9.86 us
    unnamed x23, local copies, waits for them, and re-layouts  9.2 us
    all_to_all x1, starting transfers between devices, per_device(): lax.all_to_all(weighted_terms_flat[inverse_order].astype(jnp.bfloat16), '...  7.23 us
  transfers between devices with their start and end apart: 6, of which 5 were waited for; matrix products, arithmetic and copies ran while one was open for 3% of the time, Pallas kernels for 0%

commit v1 on v0

v1 whole, which is shorter than its diff:
```python
import functools

import jax
import jax.numpy as jnp
import numpy as np
from jax import lax
from jax.experimental import pallas as pl
from jax.experimental.pallas import tpu as pltpu
from jax.sharding import PartitionSpec as P

F32 = jnp.float32
BF16 = jnp.bfloat16
MESH = pl.DeviceIdType.MESH


def dot(a, b):
    return jnp.dot(a, b, preferred_element_type=F32)


def contract(a, b, dim_a, dim_b):
    return lax.dot_general(
        a, b, (((dim_a,), (dim_b,)), ((), ())), preferred_element_type=F32
    )


def silu_of_half(z):
    return (z + z * jnp.tanh(z)).astype(BF16)


def physics_kernel(
    blocks, groups, cls_ref, win_ref, wout_ref, wflux_ref, x_hbm,
    y_hbm, flux_ref, xv, half_in, half_out, mix, in_sem, out_sem, *state
):
    zs, ss, hs = state[:blocks], state[blocks : 2 * blocks], state[2 * blocks :]
    width = blocks // groups

    def load(g):
        part = pl.ds(g * width, width)
        return pltpu.make_async_copy(x_hbm.at[part], xv.at[part], in_sem.at[g])

    def save(g):
        part = pl.ds(g * width, width)
        return pltpu.make_async_copy(xv.at[part], y_hbm.at[part], out_sem.at[g])

    for g in range(groups):
        load(g).start()
    half_in[...] = win_ref[...] * 0.5
    half_out[...] = wout_ref[...] * 0.5
    mix[...] = dot(half_in[...], half_out[...]).astype(BF16)
    for g in range(groups):
        load(g).wait()
        for i in range(g * width, (g + 1) * width):
            z = dot(half_in[...], xv[i])
            zs[i][...] = z
            h = silu_of_half(z)
            hs[i][...] = h
            ss[i][...] = h

    def update(_, carry):
        for i in range(blocks):
            z = zs[i][...] + dot(mix[...], hs[i][...])
            zs[i][...] = z
            h = silu_of_half(z)
            hs[i][...] = h
            ss[i][...] = ss[i][...] + h
        return carry

    lax.fori_loop(0, cls_ref[0] - 1, update, 0)
    for g in range(groups):
        for i in range(g * width, (g + 1) * width):
            y = (xv[i].astype(F32) + dot(half_out[...], ss[i][...])).astype(BF16)
            xv[i] = y
            flux = dot(wflux_ref[...], y)
            flux_ref[i, 0:4, :] = flux[:, :128]
            flux_ref[i, 4:8, :] = flux[:, 128:]
        save(g).start()
    for g in range(groups):
        save(g).wait()


def physics(cost_class, w_in, w_out, w_flux, atm_state):
    blocks, feat, cells = atm_state.shape
    hid = w_in.shape[0]
    groups = 4
    vmem = pl.BlockSpec(memory_space=pltpu.VMEM)
    anywhere = pl.BlockSpec(memory_space=pl.ANY)
    return pl.pallas_call(
        functools.partial(physics_kernel, blocks, groups),
        out_shape=(
            jax.ShapeDtypeStruct(atm_state.shape, BF16),
            jax.ShapeDtypeStruct((blocks, 8, 128), F32),
        ),
        in_specs=[pl.BlockSpec(memory_space=pltpu.SMEM), vmem, vmem, vmem, anywhere],
        out_specs=(anywhere, vmem),
        scratch_shapes=[
            pltpu.VMEM((blocks, feat, cells), BF16),
            pltpu.VMEM((hid, feat), BF16),
            pltpu.VMEM((feat, hid), BF16),
            pltpu.VMEM((hid, hid), BF16),
            pltpu.SemaphoreType.DMA((groups,)),
            pltpu.SemaphoreType.DMA((groups,)),
        ]
        + [pltpu.VMEM((hid, cells), F32)] * blocks
        + [pltpu.VMEM((hid, cells), BF16)] * (2 * blocks),
        compiler_params=pltpu.CompilerParams(vmem_limit_bytes=56 * 2**20),
        name="column_physics",
    )(cost_class, w_in, w_out, w_flux, atm_state)


def exchange_kernel(
    sec_count, lon_count, levels,
    index_ref, flux_hbm, weight_hbm, tracers_hbm, mask_hbm,
    next_hbm, temp_ref,
    weight, tracers, land, result, flux_in, terms, temp_out, temp_in,
    rows_bf, edge_out, west_in, east_in, halo, row_out, row_in, row_wide,
    weight_sem, tracer_sem, mask_sem, save_sem,
    flux_send, flux_recv, temp_send, temp_recv, halo_send, halo_recv,
):
    sec, lon, lat = lax.axis_index("sec"), lax.axis_index("lon"), lax.axis_index("lat")
    total = sec_count * lon_count
    place = sec * lon_count + lon
    before = lax.rem(place + total - 1, total)
    after = lax.rem(place + 1, total)
    west = (before // lon_count, lax.rem(before, lon_count), lat)
    east = (after // lon_count, lax.rem(after, lon_count), lat)
    across = (sec, lon, 1 - lat)
    ocean_rows, cells = land.shape
    pairs = ocean_rows * 4
    fields = 2 * levels
    lines = fields * ocean_rows

    weight_copies = [
        pltpu.make_async_copy(
            weight_hbm.at[pl.ds(8 * g, 8)], weight.at[pl.ds(8 * g, 8)], weight_sem.at[g]
        )
        for g in range(pairs // 8)
    ]
    tracer_copy = pltpu.make_async_copy(tracers_hbm, tracers, tracer_sem)
    mask_copy = pltpu.make_async_copy(mask_hbm, land, mask_sem)
    tracer_copy.start()
    mask_copy.start()
    for copy in weight_copies:
        copy.start()

    barrier = pltpu.get_barrier_semaphore()

    def greet(step, carry):
        peer = lax.rem(lon + step, lon_count)
        pl.semaphore_signal(barrier, inc=1, device_id=(sec, peer, lat), device_id_type=MESH)
        return carry

    for neighbour in (west, east, across):
        pl.semaphore_signal(barrier, inc=1, device_id=neighbour, device_id_type=MESH)
    lax.fori_loop(1, lon_count, greet, 0)
    pl.semaphore_wait(barrier, lon_count + 2)

    def spread_out(source, target, send_sem, recv_sem):
        def one(step, carry):
            peer = lax.rem(lon + step, lon_count)
            pltpu.make_async_remote_copy(
                src_ref=source.at[peer],
                dst_ref=target.at[lon],
                send_sem=send_sem,
                recv_sem=recv_sem,
                device_id=(sec, peer, lat),
                device_id_type=MESH,
            ).start()
            return carry

        lax.fori_loop(1, lon_count, one, 0)
        pltpu.make_async_copy(source.at[lon], target.at[lon], recv_sem).start()

    def await_bytes(ref, sem):
        pltpu.make_async_copy(ref, ref, sem).wait()

    spread_out(flux_hbm, flux_in, flux_send, flux_recv)

    tracer_copy.wait()
    mask_copy.wait()
    mask = land[...].astype(F32)
    rows_bf[0:lines, :] = tracers[...].reshape(lines, cells).astype(BF16)
    rows_bf[lines : lines + ocean_rows, :] = mask.astype(BF16)
    rows_bf[lines + ocean_rows :, :] = jnp.zeros(
        (rows_bf.shape[0] - lines - ocean_rows, cells), BF16
    )
    pick_row = lax.broadcasted_iota(jnp.int32, (16, cells), 0)
    pick_lane = lax.broadcasted_iota(jnp.int32, (16, cells), 1)
    pick = jnp.where(
        ((pick_row == 0) & (pick_lane == 0)) | ((pick_row == 1) & (pick_lane == cells - 1)), 1.0, 0.0
    ).astype(BF16)
    edge_out[...] = contract(pick, rows_bf[...], 1, 1)[:8]
    first = tracers[:, 0, :]
    last = tracers[:, ocean_rows - 1, :]
    near = jnp.where(lat == 0, last, first).astype(BF16)
    near_mask = jnp.where(lat == 0, mask[ocean_rows - 1 :], mask[:1])
    row_out[0:fields, :] = near
    row_out[fields:, :] = jnp.broadcast_to(near_mask, (row_out.shape[0] - fields, cells)).astype(
        BF16
    )

    def halo_copy(which, source, target, device):
        return pltpu.make_async_remote_copy(
            src_ref=source,
            dst_ref=target,
            send_sem=halo_send.at[which],
            recv_sem=halo_recv.at[which],
            device_id=device,
            device_id_type=MESH,
        )

    halo_copies = [
        halo_copy(0, edge_out, east_in, west),
        halo_copy(1, edge_out, west_in, east),
        halo_copy(2, row_out, row_in, across),
    ]
    for copy in halo_copies:
        copy.start()
    for copy in halo_copies:
        copy.wait_recv()

    edges = jnp.concatenate([west_in[...], east_in[...]], 0).astype(BF16)
    place_back = jnp.where(
        ((pick_row == 1) & (pick_lane == 0)) | ((pick_row == 8) & (pick_lane == cells - 1)), 1.0, 0.0
    ).astype(BF16)
    halo[...] = contract(edges, place_back, 0, 0)
    row_wide[...] = row_in[...].astype(F32)

    row_at = lax.broadcasted_iota(jnp.int32, (ocean_rows, cells), 0)
    lane_at = lax.broadcasted_iota(jnp.int32, (ocean_rows, cells), 1)
    top, bottom = row_at == 0, row_at == ocean_rows - 1
    left, right = lane_at == 0, lane_at == cells - 1

    def neighbours(value, side, line):
        return (
            jnp.where(left, side, pltpu.roll(value, 1, 1)),
            jnp.where(right, side, pltpu.roll(value, cells - 1, 1)),
            jnp.where(top, line, pltpu.roll(value, 1, 0)),
            jnp.where(bottom, line, pltpu.roll(value, ocean_rows - 1, 0)),
        )

    mask_w, mask_e, mask_n, mask_s = neighbours(
        mask, halo[lines : lines + ocean_rows, :], row_wide[fields : fields + 1, :]
    )
    mask_w = jnp.where(left & (place == 0), 0.0, mask_w) * 0.2
    mask_e = jnp.where(right & (place == total - 1), 0.0, mask_e) * 0.2
    mask_n = jnp.where(top & (lat == 0), 0.0, mask_n) * 0.2
    mask_s = jnp.where(bottom & (lat == 1), 0.0, mask_s) * 0.2
    mask_sum = mask_w + mask_e + mask_n + mask_s

    def level(field):
        return pl.ds(pl.multiple_of(field * ocean_rows, ocean_rows), ocean_rows)

    def interior(n):
        base = n * levels

        def one(k, carry):
            here, drop_above = carry
            f = base + k
            below = tracers[base + jnp.minimum(k + 1, levels - 1)]
            drop = below - here
            w, e, nn, s = neighbours(here, halo[level(f), :], row_wide[pl.ds(f, 1), :])
            change = (
                mask_w * w + mask_e * e + mask_n * nn + mask_s * s
                - mask_sum * here
                + 0.1 * (drop - drop_above)
            )
            result[f] = here + mask * change
            return below, drop

        start = tracers[base]
        lax.fori_loop(0, levels, one, (start, jnp.zeros_like(start)), unroll=4)

    interior(0)
    interior(1)

    await_bytes(flux_in, flux_recv)
    for copy in weight_copies:
        copy.wait()
    forcing = []
    for r in range(ocean_rows):
        total_flux = None
        for k in range(4):
            source = lax.rem(lax.shift_right_logical(index_ref[r, 0, k], 6), lon_count)
            tile = flux_in[source]
            lhs = jnp.concatenate([tile[0:4], tile[4:8]], 1).astype(BF16)
            part = dot(lhs, weight[4 * r + k])
            total_flux = part if total_flux is None else total_flux + part
        forcing.append(total_flux)
    flux_of = [
        jnp.concatenate([forcing[r][f : f + 1] for r in range(ocean_rows)], 0) for f in range(4)
    ]

    square = flux_of[3] * flux_of[3]
    extra = mask * (0.3 * square / (1.0 + square))
    decay = [float(v) for v in depth_fractions(levels)]
    heat = 0.5 * mask * flux_of[1]
    for n in range(2):
        base = n * levels
        jump = extra * (tracers[base + 1] - tracers[base])
        surface = result[base] + jump
        if n == 0:
            surface = surface + (0.5 * mask * flux_of[0] + decay[0] * heat)
            sst = surface
        else:
            surface = surface + 0.3 * mask * flux_of[2]
        result[base] = surface
        result[base + 1] = result[base + 1] - jump

    sst_bf = jnp.concatenate([sst, jnp.zeros_like(sst)], 0).astype(BF16)
    column = lax.broadcasted_iota(jnp.int32, (lon_count, 128), 1)
    owner = lax.broadcasted_iota(jnp.int32, (lon_count, 128), 0)
    order = jnp.zeros((lon_count, 128), F32)
    for r in range(ocean_rows):
        for k in range(4):
            p = 4 * r + k
            back = contract(sst_bf, weight[p], 1, 1)
            terms[p : p + 1, :] = back[r : r + 1]
            source = lax.rem(lax.shift_right_logical(index_ref[r, 0, k], 6), lon_count)
            order = jnp.where((column == p) & (owner == source), 1.0, order)
    terms[pairs:, :] = jnp.zeros((128 - pairs, cells), F32)
    ordered = dot(order.astype(BF16), terms[...].astype(BF16))
    temp_out[:, 0, :] = ordered[:, :128]
    temp_out[:, 1, :] = ordered[:, 128:]
    temp_out[:, 2:, :] = jnp.zeros((lon_count, 6, 128), F32)
    spread_out(temp_out, temp_in, temp_send, temp_recv)

    for k in range(1, levels):
        result[k] = result[k] + decay[k] * heat
    save = pltpu.make_async_copy(result, next_hbm, save_sem)
    save.start()
    for copy in halo_copies:
        copy.wait_send()
    await_bytes(flux_hbm.at[pl.ds(0, lon_count - 1)], flux_send)
    await_bytes(temp_in, temp_recv)
    temp_ref[:, :128] = temp_in[:, 0, :]
    temp_ref[:, 128:] = temp_in[:, 1, :]
    await_bytes(temp_out.at[pl.ds(0, lon_count - 1)], temp_send)
    save.wait()


def depth_fractions(levels):
    k = np.arange(levels, dtype=np.float64)
    return np.exp(-k / 8.0) - np.exp(-(k + 1.0) / 8.0)


def exchange(index, flux, weight, tracers, land_sea):
    sec_count, lon_count = lax.axis_size("sec"), lax.axis_size("lon")
    levels, ocean_rows, cells = tracers.shape[1:]
    pairs = ocean_rows * 4
    lines = 2 * levels * ocean_rows
    padded = -(-(lines + ocean_rows) // 128) * 128
    anywhere = pl.BlockSpec(memory_space=pl.ANY)
    next_flat, temp = pl.pallas_call(
        functools.partial(exchange_kernel, sec_count, lon_count, levels),
        out_shape=(
            jax.ShapeDtypeStruct((2 * levels, ocean_rows, cells), F32),
            jax.ShapeDtypeStruct((lon_count, cells), F32),
        ),
        in_specs=[pl.BlockSpec(memory_space=pltpu.SMEM)] + [anywhere] * 4,
        out_specs=(anywhere, pl.BlockSpec(memory_space=pltpu.VMEM)),
        scratch_shapes=[
            pltpu.VMEM((pairs, cells, cells), BF16),
            pltpu.VMEM((2 * levels, ocean_rows, cells), F32),
            pltpu.VMEM((ocean_rows, cells), jnp.int32),
            pltpu.VMEM((2 * levels, ocean_rows, cells), F32),
            pltpu.VMEM((lon_count, 8, 128), F32),
            pltpu.VMEM((128, cells), F32),
            pltpu.VMEM((lon_count, 8, 128), F32),
            pltpu.VMEM((lon_count, 8, 128), F32),
            pltpu.VMEM((padded, cells), BF16),
            pltpu.VMEM((8, padded), F32),
            pltpu.VMEM((8, padded), F32),
            pltpu.VMEM((8, padded), F32),
            pltpu.VMEM((padded, cells), F32),
            pltpu.VMEM((2 * levels + 16, cells), BF16),
            pltpu.VMEM((2 * levels + 16, cells), BF16),
            pltpu.VMEM((2 * levels + 16, cells), F32),
            pltpu.SemaphoreType.DMA((pairs // 8,)),
            pltpu.SemaphoreType.DMA,
            pltpu.SemaphoreType.DMA,
            pltpu.SemaphoreType.DMA,
            pltpu.SemaphoreType.DMA,
            pltpu.SemaphoreType.DMA,
            pltpu.SemaphoreType.DMA,
            pltpu.SemaphoreType.DMA,
            pltpu.SemaphoreType.DMA((3,)),
            pltpu.SemaphoreType.DMA((3,)),
        ],
        compiler_params=pltpu.CompilerParams(
            vmem_limit_bytes=40 * 2**20, collective_id=0, has_side_effects=True
        ),
        name="coupling_exchange",
    )(
        index,
        flux,
        weight.reshape(pairs, cells, cells),
        tracers.reshape(2 * levels, ocean_rows, cells),
        land_sea,
    )
    return next_flat.reshape(tracers.shape), temp


def per_device(
    atm_state,
    cost_class,
    w_in,
    w_out,
    w_flux,
    feeding_block_index,
    pairwise_remap_weight,
    ocean_tracers,
    land_sea,
):
    column_state_next, flux = physics(cost_class, w_in, w_out, w_flux, atm_state)
    tracer_fields_next, atmos_surface_temp = exchange(
        feeding_block_index, flux, pairwise_remap_weight, ocean_tracers, land_sea
    )
    return (column_state_next, tracer_fields_next, atmos_surface_temp)


def solution(mesh):
    return jax.shard_map(
        per_device,
        mesh=mesh,
        in_specs=(
            P(("sec", "lon", "lat"), None, None),
            P(("sec", "lon", "lat")),
            P(),
            P(),
            P(),
            P("lat", ("sec", "lon"), None),
            P("lat", ("sec", "lon"), None, None, None),
            P(None, None, "lat", ("sec", "lon")),
            P("lat", ("sec", "lon")),
        ),
        out_specs=(
            P(("sec", "lon", "lat"), None, None),
            P(None, None, "lat", ("sec", "lon")),
            P(("sec", "lon", "lat"), None),
        ),
        check_vma=False,
    )
```

time: 348 us -> 70.1 us (0.20)
  waiting for transfers between devices: 261 us -> 0 us
  Pallas kernels: 0 us -> 64.8 us
  matrix products: 20 us -> 0 us
  local copies, waits for them, and re-layouts: 24.1 us -> 4.21 us
  starting transfers between devices: 19.7 us -> 0 us
  between operations: 14.3 us -> 0.68 us
  other arithmetic: 5.76 us -> 0 us
    ppermute x4 -> x0, waiting for transfers between devices: 132 us -> none  [the longest x2 130 us: with_halo(): lax.ppermute(lax.slice_in_dim(block, 0, width, axis=dim), axis, backward)]
    all_gather x1 -> x0, waiting for transfers between devices: 127 us -> none  [per_device(): arrived_flux = lax.all_gather(fluxes, 'lon', axis=0, tiled=True)]
    pallas_call x0 -> x2, Pallas kernels: none -> 64.8 us  [the longest x1 41.5 us: physics(): pl.pallas_call(functools.partial(physics_kernel, blocks, groups), out_sha...]
    dot_general x4 -> x0, matrix products: 20 us -> none  [the longest x1 11.9 us: column_update(): jnp.einsum('fh,bhc->bfc', w_out, hidden, preferred_element_type=jnp.float32)]
    ppermute x4 -> x0, starting transfers between devices: 12.4 us -> none  [the longest x2 9.86 us: with_halo(): lax.ppermute(lax.slice_in_dim(block, block.shape[dim] - width, None, axis...]
    while x2 -> x0, local copies, waits for them, and re-layouts: 11.2 us -> none  [the longest x1 6.58 us: per_device(): lax.fori_loop(jnp.int32(0), jnp.max(cost_class), substep, atm_state)]
    all_to_all x1 -> x0, starting transfers between devices: 7.23 us -> none  [per_device(): lax.all_to_all(weighted_terms_flat[inverse_order].astype(jnp.bfloat16), '...]
    unnamed x23 -> x11, local copies, waits for them, and re-layouts: 9.2 us -> 4.21 us
  transfers between devices with their start and end apart: 6 -> 0, of which waited for: 5 -> 0; matrix products, arithmetic and copies ran while one was open for 3% -> 0% of each run, Pallas kernels for 0% -> 0%
where the time goes in v1:
time: 70.1 us; the launch traced here: 69.7 us
  Pallas kernels  64.8 us (92%)
  local copies, waits for them, and re-layouts  4.21 us (6%)
    pallas_call x1, Pallas kernels, physics(): pl.pallas_call(functools.partial(physics_kernel, blocks, groups), out_sha...  41.5 us
    pallas_call x1, Pallas kernels, exchange(): pl.pallas_call(functools.partial(exchange_kernel, sec_count, lon_count, l...  23.3 us
    unnamed x11, local copies, waits for them, and re-layouts  4.21 us

profile of v1, /device:TPU:0, one launch (start us, length us, event | category | flops | bytes accessed | tf_op | source)
XLA Modules:
  0.0 69.7 jit_solution(1893847385660359475)
XLA Ops:
  0.6 0.0 copy-start.3
  0.6 0.8 %copy.12.index_ref = s32[8,1,4]{2,1,0:T(1,128)S(1)} copy(s32[8,1,4]{0,2,1:T(4,128)} %param.14) | data formatting | bytes 256 | tf_op args[5]
  1.4 0.0 copy-start
  1.4 41.5 %column_physics.1 = (bf16[32,256,256]{2,1,0:T(8,128)(2,1)}, f32[32,8,128]{2,1,0:T(8,128)}) custom-call(s32[32]{0:T(128)} %cls_ref.1, bf16[384,256]{1,0:T(8,128)(2,1)} %win_ref.1, bf16[256,384]{1,0:T(8,128)(2,1)} %wout_ref.1, bf16[4,256]{1,0:T(4,128)(2,1)} %wflux_ref.1, bf16[32,256,256]{2,1,0:T(8,128)(2,1)} %x_hbm.1), custom_call_target="tpu_custom_call" | custom-call | tf_op jit(solution)/shard_map/column_physics/pallas_call | solution.py:87
  42.9 0.0 copy-done.3
  42.9 0.0 copy-done
  42.9 0.0 copy-start.1
  42.9 1.1 %copy-done.1 = f32[2,40,8,256]{3,2,1,0:T(8,128)S(1)} copy-done((f32[2,40,8,256]{3,2,1,0:T(8,128)S(1)}, f32[2,40,8,256]{3,2,1,0:T(8,128)}, u32[]{:S(2)}) %copy-start.1) | copy-done | bytes 655384
  44.0 0.0 copy-start.2
  44.0 0.9 %copy-done.2 = f32[32,8,128]{2,1,0:T(8,128)S(1)} copy-done((f32[32,8,128]{2,1,0:T(8,128)S(1)}, f32[32,8,128]{2,1,0:T(8,128)}, u32[]{:S(2)}) %copy-start.2) | copy-done | bytes 131096
  44.9 23.3 %coupling_exchange.1 = (f32[80,8,256]{2,1,0:T(8,128)S(1)}, f32[32,256]{1,0:T(8,128)S(1)}) custom-call(s32[8,1,4]{2,1,0:T(1,128)S(1)} %copy.12.index_ref, f32[32,8,128]{2,1,0:T(8,128)S(1)} %copy-done.2, bf16[32,256,256]{2,1,0:T(8,128)(2,1)S(1)} %bitcast.3, f32[80,8,256]{2,1,0:T(8,128)S(1)} %bitcast.5, s32[8,256]{1,0:T(8,128)S(1)} %copy-done.3), custom_call_target="tpu_custom_call" | custom-call | tf_op jit(solution)/shard_map/coupling_exchange/pallas_call | solution.py:353
  68.3 0.8 %copy.15 = f32[2,40,8,256]{3,2,1,0:T(8,128)} copy(f32[2,40,8,256]{3,2,1,0:T(8,128)S(1)} %bitcast.4) | data formatting | bytes 1310720
  69.1 0.6 copy.16
Async XLA Ops:
  0.6 42.3 %copy-start.3 = (s32[8,256]{1,0:T(8,128)S(1)}, s32[8,256]{1,0:T(8,128)}, u32[]{:S(2)}) copy-start(s32[8,256]{1,0:T(8,128)} %mask_hbm.1) | copy-start | bytes 24580
  1.4 41.5 %copy-start = (bf16[8,1,4,256,256]{4,3,2,1,0:T(8,128)(2,1)S(1)}, bf16[8,1,4,256,256]{4,3,2,1,0:T(8,128)(2,1)}, u32[]{:S(2)}) copy-start(bf16[8,1,4,256,256]{4,3,2,1,0:T(8,128)(2,1)} %param.15) | copy-start | bytes 12582916
  42.9 1.1 %copy-start.1 = (f32[2,40,8,256]{3,2,1,0:T(8,128)S(1)}, f32[2,40,8,256]{3,2,1,0:T(8,128)}, u32[]{:S(2)}) copy-start(f32[2,40,8,256]{3,2,1,0:T(8,128)} %param.16) | copy-start | bytes 1966084
  44.0 0.9 %copy-start.2 = (f32[32,8,128]{2,1,0:T(8,128)S(1)}, f32[32,8,128]{2,1,0:T(8,128)}, u32[]{:S(2)}) copy-start(f32[32,8,128]{2,1,0:T(8,128)} %get-tuple-element.8.flux_hbm) | copy-start | bytes 393220

commit v2 on v1

v2 whole, which is shorter than its diff:
```python
import functools

import jax
import jax.numpy as jnp
import numpy as np
from jax import lax
from jax.experimental import pallas as pl
from jax.experimental.pallas import tpu as pltpu
from jax.sharding import PartitionSpec as P

F32 = jnp.float32
BF16 = jnp.bfloat16
MESH = pl.DeviceIdType.MESH


def dot(a, b):
    return jnp.dot(a, b, preferred_element_type=F32)


def contract(a, b, dim_a, dim_b):
    return lax.dot_general(
        a, b, (((dim_a,), (dim_b,)), ((), ())), preferred_element_type=F32
    )


def coupled_kernel(
    sec_count, lon_count, levels, groups, longest,
    cls_ref, index_ref, win_ref, wout_ref, wflux_ref, x_hbm, weight_hbm, tracers_hbm, mask_hbm,
    y_hbm, next_hbm, temp_ref,
    xv, half_in, half_out, mix, flux_out, in_sem, out_sem,
    weight, tracers, land, result, flux_in, terms, temp_out, temp_in,
    rows_bf, edge_out, west_in, east_in, halo, row_out, row_in, row_wide,
    weight_sem, tracer_sem, mask_sem, save_sem,
    flux_send, flux_recv, temp_send, temp_recv, halo_send, halo_recv,
    *state,
):
    sec, lon, lat = lax.axis_index("sec"), lax.axis_index("lon"), lax.axis_index("lat")
    total = sec_count * lon_count
    place = sec * lon_count + lon
    before = lax.rem(place + total - 1, total)
    after = lax.rem(place + 1, total)
    west = (before // lon_count, lax.rem(before, lon_count), lat)
    east = (after // lon_count, lax.rem(after, lon_count), lat)
    across = (sec, lon, 1 - lat)
    ocean_rows, cells = land.shape
    blocks = xv.shape[0]
    zs, ss, hs = state[:blocks], state[blocks : 2 * blocks], state[2 * blocks :]
    width = blocks // groups
    pairs = ocean_rows * 4
    fields = 2 * levels
    lines = fields * ocean_rows

    weight_copies = [
        pltpu.make_async_copy(
            weight_hbm.at[pl.ds(8 * g, 8)], weight.at[pl.ds(8 * g, 8)], weight_sem.at[g]
        )
        for g in range(pairs // 8)
    ]
    tracer_copy = pltpu.make_async_copy(tracers_hbm, tracers, tracer_sem)
    mask_copy = pltpu.make_async_copy(mask_hbm, land, mask_sem)
    def load(g):
        part = pl.ds(g * width, width)
        return pltpu.make_async_copy(x_hbm.at[part], xv.at[part], in_sem.at[g])

    def save(g):
        part = pl.ds(g * width, width)
        return pltpu.make_async_copy(xv.at[part], y_hbm.at[part], out_sem.at[g])

    tracer_copy.start()
    mask_copy.start()
    for g in range(groups):
        load(g).start()
    for copy in weight_copies:
        copy.start()

    barrier = pltpu.get_barrier_semaphore()

    def greet(step, carry):
        peer = lax.rem(lon + step, lon_count)
        pl.semaphore_signal(barrier, inc=1, device_id=(sec, peer, lat), device_id_type=MESH)
        return carry

    for neighbour in (west, east, across):
        pl.semaphore_signal(barrier, inc=1, device_id=neighbour, device_id_type=MESH)
    lax.fori_loop(1, lon_count, greet, 0)

    def spread_out(source, target, send_sem, recv_sem):
        def one(step, carry):
            peer = lax.rem(lon + step, lon_count)
            pltpu.make_async_remote_copy(
                src_ref=source.at[peer],
                dst_ref=target.at[lon],
                send_sem=send_sem,
                recv_sem=recv_sem,
                device_id=(sec, peer, lat),
                device_id_type=MESH,
            ).start()
            return carry

        lax.fori_loop(1, lon_count, one, 0)
        pltpu.make_async_copy(source.at[lon], target.at[lon], recv_sem).start()

    def await_bytes(ref, sem):
        pltpu.make_async_copy(ref, ref, sem).wait()

    tracer_copy.wait()
    mask_copy.wait()
    mask = land[...].astype(F32)
    rows_bf[0:lines, :] = tracers[...].reshape(lines, cells).astype(BF16)
    rows_bf[lines : lines + ocean_rows, :] = mask.astype(BF16)
    rows_bf[lines + ocean_rows :, :] = jnp.zeros(
        (rows_bf.shape[0] - lines - ocean_rows, cells), BF16
    )
    pick_row = lax.broadcasted_iota(jnp.int32, (16, cells), 0)
    pick_lane = lax.broadcasted_iota(jnp.int32, (16, cells), 1)
    pick = jnp.where(
        ((pick_row == 0) & (pick_lane == 0)) | ((pick_row == 1) & (pick_lane == cells - 1)), 1.0, 0.0
    ).astype(BF16)
    edge_out[...] = contract(pick, rows_bf[...], 1, 1)[:8]
    first = tracers[:, 0, :]
    last = tracers[:, ocean_rows - 1, :]
    near = jnp.where(lat == 0, last, first).astype(BF16)
    near_mask = jnp.where(lat == 0, mask[ocean_rows - 1 :], mask[:1])
    row_out[0:fields, :] = near
    row_out[fields:, :] = jnp.broadcast_to(near_mask, (row_out.shape[0] - fields, cells)).astype(
        BF16
    )

    def halo_copy(which, source, target, device):
        return pltpu.make_async_remote_copy(
            src_ref=source,
            dst_ref=target,
            send_sem=halo_send.at[which],
            recv_sem=halo_recv.at[which],
            device_id=device,
            device_id_type=MESH,
        )

    halo_copies = [
        halo_copy(0, edge_out, east_in, west),
        halo_copy(1, edge_out, west_in, east),
        halo_copy(2, row_out, row_in, across),
    ]
    half_in[...] = win_ref[...] * 0.5
    half_out[...] = wout_ref[...] * 0.5
    mix[...] = dot(half_in[...], half_out[...]).astype(BF16)
    for g in range(groups):
        load(g).wait()
        for i in range(g * width, (g + 1) * width):
            z = dot(half_in[...], xv[i])
            zs[i][...] = z
            h = (z + z * jnp.tanh(z)).astype(BF16)
            hs[i][...] = h
            ss[i][...] = h

    def update(counter, carry):
        alive = jnp.full(half_in.shape[:1] + (cells,), jnp.where(cls_ref[0] > counter, 1.0, 0.0)).astype(BF16)
        for i in range(blocks):
            z = zs[i][...] + dot(mix[...], hs[i][...])
            zs[i][...] = z
            h = (z + z * jnp.tanh(z)).astype(BF16)
            hs[i][...] = h
            ss[i][...] = ss[i][...] + h * alive
        return carry

    lax.fori_loop(1, longest, update, 0)
    pl.semaphore_wait(barrier, lon_count + 2)
    for copy in halo_copies:
        copy.start()
    for i in range(blocks):
        xv[i] = (xv[i].astype(F32) + dot(half_out[...], ss[i][...])).astype(BF16)
    for g in range(groups):
        save(g).start()

    batch = 8
    for first in range(0, lon_count, batch):
        slots = [lax.rem(lon + first + i, lon_count) for i in range(batch)]
        for slot in slots:
            flux = dot(wflux_ref[...], xv[slot])
            flux_out[slot, 0:4, :] = flux[:, :128]
            flux_out[slot, 4:8, :] = flux[:, 128:]
        for i, slot in enumerate(slots):
            if first + i == 0:
                pltpu.make_async_copy(flux_out.at[slot], flux_in.at[lon], flux_recv).start()
            else:
                pltpu.make_async_remote_copy(
                    src_ref=flux_out.at[slot],
                    dst_ref=flux_in.at[lon],
                    send_sem=flux_send,
                    recv_sem=flux_recv,
                    device_id=(sec, slot, lat),
                    device_id_type=MESH,
                ).start()

    for copy in halo_copies:
        copy.wait_recv()

    edges = jnp.concatenate([west_in[...], east_in[...]], 0).astype(BF16)
    place_back = jnp.where(
        ((pick_row == 1) & (pick_lane == 0)) | ((pick_row == 8) & (pick_lane == cells - 1)), 1.0, 0.0
    ).astype(BF16)
    halo[...] = contract(edges, place_back, 0, 0)
    row_wide[...] = row_in[...].astype(F32)

    row_at = lax.broadcasted_iota(jnp.int32, (ocean_rows, cells), 0)
    lane_at = lax.broadcasted_iota(jnp.int32, (ocean_rows, cells), 1)
    top, bottom = row_at == 0, row_at == ocean_rows - 1
    left, right = lane_at == 0, lane_at == cells - 1

    def neighbours(value, side, line):
        return (
            jnp.where(left, side, pltpu.roll(value, 1, 1)),
            jnp.where(right, side, pltpu.roll(value, cells - 1, 1)),
            jnp.where(top, line, pltpu.roll(value, 1, 0)),
            jnp.where(bottom, line, pltpu.roll(value, ocean_rows - 1, 0)),
        )

    mask_w, mask_e, mask_n, mask_s = neighbours(
        mask, halo[lines : lines + ocean_rows, :], row_wide[fields : fields + 1, :]
    )
    mask_w = jnp.where(left & (place == 0), 0.0, mask_w) * 0.2
    mask_e = jnp.where(right & (place == total - 1), 0.0, mask_e) * 0.2
    mask_n = jnp.where(top & (lat == 0), 0.0, mask_n) * 0.2
    mask_s = jnp.where(bottom & (lat == 1), 0.0, mask_s) * 0.2
    mask_sum = mask_w + mask_e + mask_n + mask_s

    def sideways(field, here):
        w, e, n, s = neighbours(
            here,
            halo[pl.ds(pl.multiple_of(field * ocean_rows, ocean_rows), ocean_rows), :],
            row_wide[pl.ds(field, 1), :],
        )
        return mask_w * w + mask_e * e + mask_n * n + mask_s * s - mask_sum * here

    surface = [tracers[0], tracers[levels]]
    calm = [
        here + mask * sideways(field, here)
        for field, here in zip((0, levels), surface)
    ]

    await_bytes(flux_in, flux_recv)
    for copy in weight_copies:
        copy.wait()
    forcing = []
    for r in range(ocean_rows):
        total_flux = None
        for k in range(4):
            source = lax.rem(lax.shift_right_logical(index_ref[k, r], 6), lon_count)
            tile = flux_in[source]
            lhs = jnp.concatenate([tile[0:4], tile[4:8]], 1).astype(BF16)
            part = dot(lhs, weight[4 * r + k])
            total_flux = part if total_flux is None else total_flux + part
        forcing.append(total_flux)
    flux_of = [
        jnp.concatenate([forcing[r][f : f + 1] for r in range(ocean_rows)], 0) for f in range(4)
    ]

    square = flux_of[3] * flux_of[3]
    top_mixing = mask * (0.1 + 0.3 * square / (1.0 + square))
    ratio = float(np.exp(-1.0 / 8.0))
    heat = (0.5 * (1.0 - ratio)) * (mask * flux_of[1])
    second = [tracers[1], tracers[levels + 1]]
    descent = [top_mixing * (b - a) for a, b in zip(surface, second)]
    sst = calm[0] + descent[0] + (0.5 * mask * flux_of[0] + heat)
    result[0] = sst
    result[levels] = calm[1] + descent[1] + 0.3 * mask * flux_of[2]

    sst_bf = jnp.concatenate([sst, jnp.zeros_like(sst)], 0).astype(BF16)
    column = lax.broadcasted_iota(jnp.int32, (lon_count, 128), 1)
    owner = lax.broadcasted_iota(jnp.int32, (lon_count, 128), 0)
    order = jnp.zeros((lon_count, 128), F32)
    for r in range(ocean_rows):
        for k in range(4):
            p = 4 * r + k
            back = contract(sst_bf, weight[p], 1, 1)
            terms[p : p + 1, :] = back[r : r + 1]
            source = lax.rem(lax.shift_right_logical(index_ref[k, r], 6), lon_count)
            order = jnp.where((column == p) & (owner == source), 1.0, order)
    terms[pairs:, :] = jnp.zeros((128 - pairs, cells), F32)
    ordered = dot(order.astype(BF16), terms[...].astype(BF16))
    temp_out[:, 0, :] = ordered[:, :128]
    temp_out[:, 1, :] = ordered[:, 128:]
    spread_out(temp_out, temp_in, temp_send, temp_recv)

    mixing = 0.1 * mask

    def deeper(k, carry):
        warm, warm_flux, salt, salt_flux, heat = carry
        lower = jnp.minimum(k + 1, levels - 1)
        heat = heat * ratio
        out = []
        for n, here, above in ((0, warm, warm_flux), (1, salt, salt_flux)):
            base = n * levels
            below = tracers[base + lower]
            flux = mixing * (below - here)
            new = here + mask * sideways(base + k, here) + (flux - above)
            result[base + k] = new + heat if n == 0 else new
            out += [below, flux]
        return (*out, heat)

    lax.fori_loop(
        1, levels, deeper, (second[0], descent[0], second[1], descent[1], heat), unroll=3
    )
    save_next = pltpu.make_async_copy(result, next_hbm, save_sem)
    save_next.start()
    for copy in halo_copies:
        copy.wait_send()
    await_bytes(flux_out.at[pl.ds(0, lon_count - 1)], flux_send)
    await_bytes(temp_in, temp_recv)
    temp_ref[:, :128] = temp_in[:, 0, :]
    temp_ref[:, 128:] = temp_in[:, 1, :]
    await_bytes(temp_out.at[pl.ds(0, lon_count - 1)], temp_send)
    save_next.wait()
    for g in range(groups):
        save(g).wait()


def in_hbm(array):
    return pltpu.with_memory_space_constraint(array, pltpu.HBM)


def coupled(
    cost_class, index, w_in, w_out, w_flux, atm_state, weight, tracers, land_sea
):
    sec_count, lon_count = lax.axis_size("sec"), lax.axis_size("lon")
    levels, ocean_rows, cells = tracers.shape[1:]
    blocks, feat = atm_state.shape[:2]
    hid = w_in.shape[0]
    longest, groups = 8, 4
    pairs = ocean_rows * 4
    fields = 2 * levels
    lines = fields * ocean_rows
    padded = -(-(lines + ocean_rows) // 128) * 128
    anywhere = pl.BlockSpec(memory_space=pl.ANY)
    hbm = pl.BlockSpec(memory_space=pltpu.HBM)
    smem = pl.BlockSpec(memory_space=pltpu.SMEM)
    vmem = pl.BlockSpec(memory_space=pltpu.VMEM)
    state, next_flat, temp = pl.pallas_call(
        functools.partial(coupled_kernel, sec_count, lon_count, levels, groups, longest),
        out_shape=(
            pltpu.VMEM(atm_state.shape, BF16),
            pltpu.VMEM((fields, ocean_rows, cells), F32),
            pltpu.VMEM((lon_count, cells), F32),
        ),
        in_specs=[smem, smem, vmem, vmem, vmem, hbm, hbm, hbm, hbm],
        out_specs=(anywhere, anywhere, vmem),
        scratch_shapes=[
            pltpu.VMEM((blocks, feat, cells), BF16),
            pltpu.VMEM((hid, feat), BF16),
            pltpu.VMEM((feat, hid), BF16),
            pltpu.VMEM((hid, hid), BF16),
            pltpu.VMEM((lon_count, 8, 128), F32),
            pltpu.SemaphoreType.DMA((groups,)),
            pltpu.SemaphoreType.DMA((groups,)),
            pltpu.VMEM((pairs, cells, cells), BF16),
            pltpu.VMEM((fields, ocean_rows, cells), F32),
            pltpu.VMEM((ocean_rows, cells), jnp.int32),
            pltpu.VMEM((fields, ocean_rows, cells), F32),
            pltpu.VMEM((lon_count, 8, 128), F32),
            pltpu.VMEM((128, cells), F32),
            pltpu.VMEM((lon_count, 2, 128), F32),
            pltpu.VMEM((lon_count, 2, 128), F32),
            pltpu.VMEM((padded, cells), BF16),
            pltpu.VMEM((8, padded), F32),
            pltpu.VMEM((8, padded), F32),
            pltpu.VMEM((8, padded), F32),
            pltpu.VMEM((padded, cells), F32),
            pltpu.VMEM((fields + 16, cells), BF16),
            pltpu.VMEM((fields + 16, cells), BF16),
            pltpu.VMEM((fields + 16, cells), F32),
            pltpu.SemaphoreType.DMA((pairs // 8,)),
            pltpu.SemaphoreType.DMA,
            pltpu.SemaphoreType.DMA,
            pltpu.SemaphoreType.DMA,
            pltpu.SemaphoreType.DMA,
            pltpu.SemaphoreType.DMA,
            pltpu.SemaphoreType.DMA,
            pltpu.SemaphoreType.DMA,
            pltpu.SemaphoreType.DMA((3,)),
            pltpu.SemaphoreType.DMA((3,)),
        ]
        + [pltpu.VMEM((hid, cells), F32)] * blocks
        + [pltpu.VMEM((hid, cells), BF16)] * (2 * blocks),
        compiler_params=pltpu.CompilerParams(
            vmem_limit_bytes=50 * 2**20, collective_id=0, has_side_effects=True
        ),
        name="coupled_step",
    )(
        cost_class,
        index[:, 0].T,
        w_in,
        w_out,
        w_flux,
        in_hbm(atm_state),
        in_hbm(weight.reshape(pairs, cells, cells)),
        in_hbm(tracers.reshape(fields, ocean_rows, cells)),
        in_hbm(land_sea),
    )
    return state, next_flat.reshape(tracers.shape), temp


def per_device(
    atm_state,
    cost_class,
    w_in,
    w_out,
    w_flux,
    feeding_block_index,
    pairwise_remap_weight,
    ocean_tracers,
    land_sea,
):
    return coupled(
        cost_class,
        feeding_block_index,
        w_in,
        w_out,
        w_flux,
        atm_state,
        pairwise_remap_weight,
        ocean_tracers,
        land_sea,
    )


def solution(mesh):
    return jax.shard_map(
        per_device,
        mesh=mesh,
        in_specs=(
            P(("sec", "lon", "lat"), None, None),
            P(("sec", "lon", "lat")),
            P(),
            P(),
            P(),
            P("lat", ("sec", "lon"), None),
            P("lat", ("sec", "lon"), None, None, None),
            P(None, None, "lat", ("sec", "lon")),
            P("lat", ("sec", "lon")),
        ),
        out_specs=(
            P(("sec", "lon", "lat"), None, None),
            P(None, None, "lat", ("sec", "lon")),
            P(("sec", "lon", "lat"), None),
        ),
        check_vma=False,
    )
```

time: 70.1 us -> 55.2 us (0.79)
  Pallas kernels: 64.8 us -> 51 us
  local copies, waits for them, and re-layouts: 4.21 us -> 3.47 us
    pallas_call x2 -> x1, Pallas kernels: 64.8 us -> 51 us  [coupled(): pl.pallas_call(functools.partial(coupled_kernel, sec_count, lon_count, le...]
    unnamed x11 -> x3, local copies, waits for them, and re-layouts: 4.21 us -> 3.47 us
where the time goes in v2:
time: 55.2 us; the launch traced here: 55.1 us
  Pallas kernels  51 us (92%)
  local copies, waits for them, and re-layouts  3.47 us (6%)
  between operations  0.64 us (1%)
    pallas_call x1, Pallas kernels, coupled(): pl.pallas_call(functools.partial(coupled_kernel, sec_count, lon_count, le...  51 us
    unnamed x3, local copies, waits for them, and re-layouts  3.47 us

profile of v2, /device:TPU:0, one launch (start us, length us, event | category | flops | bytes accessed | tf_op | source)
XLA Modules:
  0.0 55.1 jit_solution(8676098504332793067)
XLA Ops:
  0.6 51.0 %coupled_step.1 = (bf16[32,256,256]{2,1,0:T(8,128)(2,1)S(1)}, f32[80,8,256]{2,1,0:T(8,128)S(1)}, f32[32,256]{1,0:T(8,128)S(1)}) custom-call(s32[32]{0:T(128)} %cls_ref.1, s32[4,8]{1,0:T(4,128)} %bitcast.9, bf16[384,256]{1,0:T(8,128)(2,1)} %win_ref.1, bf16[256,384]{1,0:T(8,128)(2,1)} %wout_ref.1, bf16[4,256]{1,0:T(4,128)(2,1)} %wflux_ref.1, ...), custom_call_target="tpu_custom_call" | custom-call | tf_op jit(solution)/shard_map/coupled_step/pallas_call | solution.py:338
  51.6 2.0 %copy.15 = bf16[32,256,256]{2,1,0:T(8,128)(2,1)} copy(bf16[32,256,256]{2,1,0:T(8,128)(2,1)S(1)} %get-tuple-element.9) | data formatting | bytes 8388608
  53.6 0.8 %copy.16 = f32[2,40,8,256]{3,2,1,0:T(8,128)} copy(f32[2,40,8,256]{3,2,1,0:T(8,128)S(1)} %bitcast.6) | data formatting | bytes 1310720
  54.5 0.6 %copy.17 = f32[32,256]{1,0:T(8,128)} copy(f32[32,256]{1,0:T(8,128)S(1)} %get-tuple-element.11) | data formatting | bytes 65536

commit v3 on v2

--- a/solution.py
+++ b/solution.py
@@ -26,9 +26,9 @@
 def coupled_kernel(
     sec_count, lon_count, levels, groups, longest,
     cls_ref, index_ref, win_ref, wout_ref, wflux_ref, x_hbm, weight_hbm, tracers_hbm, mask_hbm,
-    y_hbm, next_hbm, temp_ref,
-    xv, half_in, half_out, mix, flux_out, in_sem, out_sem,
-    weight, tracers, land, result, flux_in, terms, temp_out, temp_in,
+    y_hbm, next_hbm, temp_in,
+    xv, half_in, half_out, mix, flux_mix, flux_out, in_sem, out_sem, w_sem,
+    weight, tracers, land, result, flux_in, terms, temp_out,
     rows_bf, edge_out, west_in, east_in, halo, row_out, row_in, row_wide,
     weight_sem, tracer_sem, mask_sem, save_sem,
     flux_send, flux_recv, temp_send, temp_recv, halo_send, halo_recv,
@@ -66,12 +66,15 @@
         part = pl.ds(g * width, width)
         return pltpu.make_async_copy(xv.at[part], y_hbm.at[part], out_sem.at[g])
 
+    hid = wout_ref.shape[1]
+    w_in_copy = pltpu.make_async_copy(win_ref, half_in.at[pl.ds(0, hid)], w_sem.at[0])
+    w_out_copy = pltpu.make_async_copy(wout_ref, half_out, w_sem.at[1])
+    w_in_copy.start()
+    w_out_copy.start()
     tracer_copy.start()
     mask_copy.start()
     for g in range(groups):
         load(g).start()
-    for copy in weight_copies:
-        copy.start()
 
     barrier = pltpu.get_barrier_semaphore()
 
@@ -84,9 +87,23 @@
         pl.semaphore_signal(barrier, inc=1, device_id=neighbour, device_id_type=MESH)
     lax.fori_loop(1, lon_count, greet, 0)
 
+    line = 4
+    plane = line * line
+    at_z, at_y, at_x = lon // plane, lax.rem(lon // line, line), lax.rem(lon, line)
+
+    def hops(step):
+        dy, dx = step // line % line, step % line
+        return step // plane + min(dy, line - dy) + min(dx, line - dx)
+
+    peers = [
+        lax.rem(at_z + step // plane, lon_count // plane) * plane
+        + lax.rem(at_y + step // line, line) * line
+        + lax.rem(at_x + step, line)
+        for step in sorted(range(1, lon_count), key=hops, reverse=True)
+    ]
+
     def spread_out(source, target, send_sem, recv_sem):
-        def one(step, carry):
-            peer = lax.rem(lon + step, lon_count)
+        for peer in peers:
             pltpu.make_async_remote_copy(
                 src_ref=source.at[peer],
                 dst_ref=target.at[lon],
@@ -95,9 +112,6 @@
                 device_id=(sec, peer, lat),
                 device_id_type=MESH,
             ).start()
-            return carry
-
-        lax.fori_loop(1, lon_count, one, 0)
         pltpu.make_async_copy(source.at[lon], target.at[lon], recv_sem).start()
 
     def await_bytes(ref, sem):
@@ -141,20 +155,32 @@
         halo_copy(1, edge_out, west_in, east),
         halo_copy(2, row_out, row_in, across),
     ]
-    half_in[...] = win_ref[...] * 0.5
-    half_out[...] = wout_ref[...] * 0.5
-    mix[...] = dot(half_in[...], half_out[...]).astype(BF16)
+    flux_rows = wflux_ref[...].astype(F32)
+    flux_rows = jnp.concatenate([flux_rows, jnp.zeros((12, flux_rows.shape[1]), F32)], 0).astype(BF16)
+    w_in_copy.wait()
+    half_in[0:hid, :] = half_in[0:hid, :] * 0.5
+    half_in[hid:, :] = flux_rows
+    w_out_copy.wait()
+    half_out[...] = half_out[...] * 0.5
+    mix[...] = dot(half_in[0:hid, :], half_out[...]).astype(BF16)
+    flux_mix[...] = dot(flux_rows, half_out[...]).astype(BF16)
     for g in range(groups):
         load(g).wait()
         for i in range(g * width, (g + 1) * width):
-            z = dot(half_in[...], xv[i])
+            both = dot(half_in[...], xv[i])
+            z = both[:hid]
+            flux_out[i, 0:4, :] = both[hid : hid + 4, :128]
+            flux_out[i, 4:8, :] = both[hid : hid + 4, 128:]
             zs[i][...] = z
             h = (z + z * jnp.tanh(z)).astype(BF16)
             hs[i][...] = h
             ss[i][...] = h
 
+    for copy in weight_copies:
+        copy.start()
+
     def update(counter, carry):
-        alive = jnp.full(half_in.shape[:1] + (cells,), jnp.where(cls_ref[0] > counter, 1.0, 0.0)).astype(BF16)
+        alive = jnp.full((hid, cells), jnp.where(cls_ref[0] > counter, 1.0, 0.0)).astype(BF16)
         for i in range(blocks):
             z = zs[i][...] + dot(mix[...], hs[i][...])
             zs[i][...] = z
@@ -168,29 +194,15 @@
     for copy in halo_copies:
         copy.start()
     for i in range(blocks):
+        flux = dot(flux_mix[...], ss[i][...])
+        flux_out[i, 0:4, :] = flux_out[i, 0:4, :] + flux[:4, :128]
+        flux_out[i, 4:8, :] = flux_out[i, 4:8, :] + flux[:4, 128:]
+    spread_out(flux_out, flux_in, flux_send, flux_recv)
+
+    for i in range(blocks):
         xv[i] = (xv[i].astype(F32) + dot(half_out[...], ss[i][...])).astype(BF16)
     for g in range(groups):
         save(g).start()
-
-    batch = 8
-    for first in range(0, lon_count, batch):
-        slots = [lax.rem(lon + first + i, lon_count) for i in range(batch)]
-        for slot in slots:
-            flux = dot(wflux_ref[...], xv[slot])
-            flux_out[slot, 0:4, :] = flux[:, :128]
-            flux_out[slot, 4:8, :] = flux[:, 128:]
-        for i, slot in enumerate(slots):
-            if first + i == 0:
-                pltpu.make_async_copy(flux_out.at[slot], flux_in.at[lon], flux_recv).start()
-            else:
-                pltpu.make_async_remote_copy(
-                    src_ref=flux_out.at[slot],
-                    dst_ref=flux_in.at[lon],
-                    send_sem=flux_send,
-                    recv_sem=flux_recv,
-                    device_id=(sec, slot, lat),
-                    device_id_type=MESH,
-                ).start()
 
     for copy in halo_copies:
         copy.wait_recv()
@@ -307,8 +319,6 @@
         copy.wait_send()
     await_bytes(flux_out.at[pl.ds(0, lon_count - 1)], flux_send)
     await_bytes(temp_in, temp_recv)
-    temp_ref[:, :128] = temp_in[:, 0, :]
-    temp_ref[:, 128:] = temp_in[:, 1, :]
     await_bytes(temp_out.at[pl.ds(0, lon_count - 1)], temp_send)
     save_next.wait()
     for g in range(groups):
@@ -317,6 +327,44 @@
 
 def in_hbm(array):
     return pltpu.with_memory_space_constraint(array, pltpu.HBM)
+
+
+def store_kernel(parts, state, following, temp, state_out, following_out, temp_out, rows, sem):
+    width = state.shape[0] // parts
+    copies = [
+        pltpu.make_async_copy(
+            state.at[pl.ds(g * width, width)], state_out.at[pl.ds(g * width, width)], sem.at[g]
+        )
+        for g in range(parts)
+    ]
+    copies.append(pltpu.make_async_copy(following, following_out, sem.at[parts]))
+    for copy in copies:
+        copy.start()
+    rows[:, :128] = temp[:, 0, :]
+    rows[:, 128:] = temp[:, 1, :]
+    copies.append(pltpu.make_async_copy(rows, temp_out, sem.at[parts + 1]))
+    copies[-1].start()
+    for copy in copies:
+        copy.wait()
+
+
+def store(state, following, temp):
+    parts = 4
+    rows = (temp.shape[0], temp.shape[1] * temp.shape[2])
+    anywhere = pl.BlockSpec(memory_space=pl.ANY)
+    return pl.pallas_call(
+        functools.partial(store_kernel, parts),
+        out_shape=(
+            pltpu.HBM(state.shape, state.dtype),
+            pltpu.HBM(following.shape, following.dtype),
+            pltpu.HBM(rows, temp.dtype),
+        ),
+        in_specs=[anywhere, anywhere, pl.BlockSpec(memory_space=pltpu.VMEM)],
+        out_specs=(anywhere,) * 3,
+        scratch_shapes=[pltpu.VMEM(rows, temp.dtype), pltpu.SemaphoreType.DMA((parts + 2,))],
+        compiler_params=pltpu.CompilerParams(vmem_limit_bytes=2 * 2**20),
+        name="store_results",
+    )(state, following, temp)
 
 
 def coupled(
@@ -340,25 +388,26 @@
         out_shape=(
             pltpu.VMEM(atm_state.shape, BF16),
             pltpu.VMEM((fields, ocean_rows, cells), F32),
-            pltpu.VMEM((lon_count, cells), F32),
+            pltpu.VMEM((lon_count, 2, 128), F32),
         ),
-        in_specs=[smem, smem, vmem, vmem, vmem, hbm, hbm, hbm, hbm],
-        out_specs=(anywhere, anywhere, vmem),
+        in_specs=[smem, smem, hbm, hbm, vmem, hbm, hbm, hbm, hbm],
+        out_specs=(anywhere, anywhere, anywhere),
         scratch_shapes=[
             pltpu.VMEM((blocks, feat, cells), BF16),
-            pltpu.VMEM((hid, feat), BF16),
+            pltpu.VMEM((hid + 16, feat), BF16),
             pltpu.VMEM((feat, hid), BF16),
             pltpu.VMEM((hid, hid), BF16),
+            pltpu.VMEM((16, hid), BF16),
             pltpu.VMEM((lon_count, 8, 128), F32),
             pltpu.SemaphoreType.DMA((groups,)),
             pltpu.SemaphoreType.DMA((groups,)),
+            pltpu.SemaphoreType.DMA((2,)),
             pltpu.VMEM((pairs, cells, cells), BF16),
             pltpu.VMEM((fields, ocean_rows, cells), F32),
             pltpu.VMEM((ocean_rows, cells), jnp.int32),
             pltpu.VMEM((fields, ocean_rows, cells), F32),
             pltpu.VMEM((lon_count, 8, 128), F32),
             pltpu.VMEM((128, cells), F32),
-            pltpu.VMEM((lon_count, 2, 128), F32),
             pltpu.VMEM((lon_count, 2, 128), F32),
             pltpu.VMEM((padded, cells), BF16),
             pltpu.VMEM((8, padded), F32),
@@ -388,14 +437,15 @@
     )(
         cost_class,
         index[:, 0].T,
-        w_in,
-        w_out,
+        in_hbm(w_in),
+        in_hbm(w_out),
         w_flux,
         in_hbm(atm_state),
         in_hbm(weight.reshape(pairs, cells, cells)),
         in_hbm(tracers.reshape(fields, ocean_rows, cells)),
         in_hbm(land_sea),
     )
+    state, next_flat, temp = store(state, next_flat, temp)
     return state, next_flat.reshape(tracers.shape), temp
 
 

time: 55.2 us -> 51.7 us (0.937)
  local copies, waits for them, and re-layouts: 3.47 us -> 0 us
    unnamed x3 -> x0, local copies, waits for them, and re-layouts: 3.47 us -> none
    pallas_call x1, Pallas kernels: 51 us -> 48.6 us  [coupled(): pl.pallas_call(functools.partial(coupled_kernel, sec_count, lon_count, le...]
    pallas_call x0 -> x1, Pallas kernels: none -> 2.27 us  [store(): pl.pallas_call(functools.partial(store_kernel, parts), out_shape=(pltpu.H...]
where the time goes in v3:
time: 51.7 us; the launch traced here: 51.5 us
  Pallas kernels  50.9 us (98%)
  between operations  0.64 us (1%)
    pallas_call x1, Pallas kernels, coupled(): pl.pallas_call(functools.partial(coupled_kernel, sec_count, lon_count, le...  48.6 us
    pallas_call x1, Pallas kernels, store(): pl.pallas_call(functools.partial(store_kernel, parts), out_shape=(pltpu.H...  2.27 us

profile of v3, /device:TPU:0, one launch (start us, length us, event | category | flops | bytes accessed | tf_op | source)
XLA Modules:
  0.0 51.5 jit_solution(13694464816401358363)
XLA Ops:
  0.6 48.6 %coupled_step.1 = (bf16[32,256,256]{2,1,0:T(8,128)(2,1)S(1)}, f32[80,8,256]{2,1,0:T(8,128)S(1)}, f32[32,2,128]{2,1,0:T(2,128)S(1)}) custom-call(s32[32]{0:T(128)} %cls_ref.1, s32[4,8]{1,0:T(4,128)} %bitcast.8, bf16[384,256]{1,0:T(8,128)(2,1)} %win_ref.1, bf16[256,384]{1,0:T(8,128)(2,1)} %wout_ref.1, bf16[4,256]{1,0:T(4,128)(2,1)} %wflux_ref.1, ...), custom_call_target="tpu_custom_call" | custom-call | tf_op jit(solution)/shard_map/coupled_step/pallas_call | solution.py:386
  49.2 2.3 %store_results.1 = (bf16[32,256,256]{2,1,0:T(8,128)(2,1)}, f32[80,8,256]{2,1,0:T(8,128)}, f32[32,256]{1,0:T(8,128)}) custom-call(bf16[32,256,256]{2,1,0:T(8,128)(2,1)S(1)} %get-tuple-element.9.state, f32[80,8,256]{2,1,0:T(8,128)S(1)} %get-tuple-element.10.following, f32[32,2,128]{2,1,0:T(2,128)S(1)} %get-tuple-element.11.temp), custom_call_target="tpu_custom_call" | custom-call | tf_op jit(solution)/shard_map/store_results/pallas_call | solution.py:355

commit v4 on v3

--- a/solution.py
+++ b/solution.py
@@ -374,7 +374,7 @@
     levels, ocean_rows, cells = tracers.shape[1:]
     blocks, feat = atm_state.shape[:2]
     hid = w_in.shape[0]
-    longest, groups = 8, 4
+    longest, groups = 8, 2
     pairs = ocean_rows * 4
     fields = 2 * levels
     lines = fields * ocean_rows

time: 51.7 us -> 51 us (0.986)
  Pallas kernels: 50.9 us -> 50.2 us
    pallas_call x1, Pallas kernels: 48.6 us -> 48 us  [coupled(): pl.pallas_call(functools.partial(coupled_kernel, sec_count, lon_count, le...]
where the time goes in v4:
time: 51 us; the launch traced here: 50.9 us
  Pallas kernels  50.2 us (98%)
  between operations  0.64 us (1%)
    pallas_call x1, Pallas kernels, coupled(): pl.pallas_call(functools.partial(coupled_kernel, sec_count, lon_count, le...  48 us
    pallas_call x1, Pallas kernels, store(): pl.pallas_call(functools.partial(store_kernel, parts), out_shape=(pltpu.H...  2.27 us

profile of v4, /device:TPU:0, one launch (start us, length us, event | category | flops | bytes accessed | tf_op | source)
XLA Modules:
  0.0 50.9 jit_solution(18160752561561466575)
XLA Ops:
  0.6 48.0 %coupled_step.1 = (bf16[32,256,256]{2,1,0:T(8,128)(2,1)S(1)}, f32[80,8,256]{2,1,0:T(8,128)S(1)}, f32[32,2,128]{2,1,0:T(2,128)S(1)}) custom-call(s32[32]{0:T(128)} %cls_ref.1, s32[4,8]{1,0:T(4,128)} %bitcast.8, bf16[384,256]{1,0:T(8,128)(2,1)} %win_ref.1, bf16[256,384]{1,0:T(8,128)(2,1)} %wout_ref.1, bf16[4,256]{1,0:T(4,128)(2,1)} %wflux_ref.1, ...), custom_call_target="tpu_custom_call" | custom-call | tf_op jit(solution)/shard_map/coupled_step/pallas_call | solution.py:386
  48.6 2.3 %store_results.1 = (bf16[32,256,256]{2,1,0:T(8,128)(2,1)}, f32[80,8,256]{2,1,0:T(8,128)}, f32[32,256]{1,0:T(8,128)}) custom-call(bf16[32,256,256]{2,1,0:T(8,128)(2,1)S(1)} %get-tuple-element.9.state, f32[80,8,256]{2,1,0:T(8,128)S(1)} %get-tuple-element.10.following, f32[32,2,128]{2,1,0:T(2,128)S(1)} %get-tuple-element.11.temp), custom_call_target="tpu_custom_call" | custom-call | tf_op jit(solution)/shard_map/store_results/pallas_call | solution.py:355

commit v5 on v4

--- a/solution.py
+++ b/solution.py
@@ -169,8 +169,7 @@
         for i in range(g * width, (g + 1) * width):
             both = dot(half_in[...], xv[i])
             z = both[:hid]
-            flux_out[i, 0:4, :] = both[hid : hid + 4, :128]
-            flux_out[i, 4:8, :] = both[hid : hid + 4, 128:]
+            flux_out[i] = both[hid : hid + 4]
             zs[i][...] = z
             h = (z + z * jnp.tanh(z)).astype(BF16)
             hs[i][...] = h
@@ -195,8 +194,7 @@
         copy.start()
     for i in range(blocks):
         flux = dot(flux_mix[...], ss[i][...])
-        flux_out[i, 0:4, :] = flux_out[i, 0:4, :] + flux[:4, :128]
-        flux_out[i, 4:8, :] = flux_out[i, 4:8, :] + flux[:4, 128:]
+        flux_out[i] = flux_out[i] + flux[:4]
     spread_out(flux_out, flux_in, flux_send, flux_recv)
 
     for i in range(blocks):
@@ -249,6 +247,16 @@
         here + mask * sideways(field, here)
         for field, here in zip((0, levels), surface)
     ]
+
+    column = lax.broadcasted_iota(jnp.int32, (lon_count, 128), 1)
+    owner = lax.broadcasted_iota(jnp.int32, (lon_count, 128), 0)
+    order = jnp.zeros((lon_count, 128), F32)
+    for r in range(ocean_rows):
+        for k in range(4):
+            source = lax.rem(lax.shift_right_logical(index_ref[k, r], 6), lon_count)
+            order = jnp.where((column == 4 * r + k) & (owner == source), 1.0, order)
+    order = order.astype(BF16)
+    terms[pairs:, :] = jnp.zeros((128 - pairs, cells), F32)
 
     await_bytes(flux_in, flux_recv)
     for copy in weight_copies:
@@ -258,8 +266,7 @@
         total_flux = None
         for k in range(4):
             source = lax.rem(lax.shift_right_logical(index_ref[k, r], 6), lon_count)
-            tile = flux_in[source]
-            lhs = jnp.concatenate([tile[0:4], tile[4:8]], 1).astype(BF16)
+            lhs = flux_in[source].astype(BF16)
             part = dot(lhs, weight[4 * r + k])
             total_flux = part if total_flux is None else total_flux + part
         forcing.append(total_flux)
@@ -278,18 +285,12 @@
     result[levels] = calm[1] + descent[1] + 0.3 * mask * flux_of[2]
 
     sst_bf = jnp.concatenate([sst, jnp.zeros_like(sst)], 0).astype(BF16)
-    column = lax.broadcasted_iota(jnp.int32, (lon_count, 128), 1)
-    owner = lax.broadcasted_iota(jnp.int32, (lon_count, 128), 0)
-    order = jnp.zeros((lon_count, 128), F32)
     for r in range(ocean_rows):
         for k in range(4):
             p = 4 * r + k
             back = contract(sst_bf, weight[p], 1, 1)
             terms[p : p + 1, :] = back[r : r + 1]
-            source = lax.rem(lax.shift_right_logical(index_ref[k, r], 6), lon_count)
-            order = jnp.where((column == p) & (owner == source), 1.0, order)
-    terms[pairs:, :] = jnp.zeros((128 - pairs, cells), F32)
-    ordered = dot(order.astype(BF16), terms[...].astype(BF16))
+    ordered = dot(order, terms[...].astype(BF16))
     temp_out[:, 0, :] = ordered[:, :128]
     temp_out[:, 1, :] = ordered[:, 128:]
     spread_out(temp_out, temp_in, temp_send, temp_recv)
@@ -398,7 +399,7 @@
             pltpu.VMEM((feat, hid), BF16),
             pltpu.VMEM((hid, hid), BF16),
             pltpu.VMEM((16, hid), BF16),
-            pltpu.VMEM((lon_count, 8, 128), F32),
+            pltpu.VMEM((lon_count, 4, cells), F32),
             pltpu.SemaphoreType.DMA((groups,)),
             pltpu.SemaphoreType.DMA((groups,)),
             pltpu.SemaphoreType.DMA((2,)),
@@ -406,7 +407,7 @@
             pltpu.VMEM((fields, ocean_rows, cells), F32),
             pltpu.VMEM((ocean_rows, cells), jnp.int32),
             pltpu.VMEM((fields, ocean_rows, cells), F32),
-            pltpu.VMEM((lon_count, 8, 128), F32),
+            pltpu.VMEM((lon_count, 4, cells), F32),
             pltpu.VMEM((128, cells), F32),
             pltpu.VMEM((lon_count, 2, 128), F32),
             pltpu.VMEM((padded, cells), BF16),

time: 51 us -> 51.2 us (level)
  no operation moved by 1% of the time
where the time goes in v5:
time: 51.2 us; the launch traced here: 51.1 us
  Pallas kernels  50.4 us (98%)
  between operations  0.64 us (1%)
    pallas_call x1, Pallas kernels, coupled(): pl.pallas_call(functools.partial(coupled_kernel, sec_count, lon_count, le...  48.1 us
    pallas_call x1, Pallas kernels, store(): pl.pallas_call(functools.partial(store_kernel, parts), out_shape=(pltpu.H...  2.27 us

profile of v5, /device:TPU:0, one launch (start us, length us, event | category | flops | bytes accessed | tf_op | source)
XLA Modules:
  0.0 51.1 jit_solution(13965210535896446656)
XLA Ops:
  0.6 48.1 %coupled_step.1 = (bf16[32,256,256]{2,1,0:T(8,128)(2,1)S(1)}, f32[80,8,256]{2,1,0:T(8,128)S(1)}, f32[32,2,128]{2,1,0:T(2,128)S(1)}) custom-call(s32[32]{0:T(128)} %cls_ref.1, s32[4,8]{1,0:T(4,128)} %bitcast.8, bf16[384,256]{1,0:T(8,128)(2,1)} %win_ref.1, bf16[256,384]{1,0:T(8,128)(2,1)} %wout_ref.1, bf16[4,256]{1,0:T(4,128)(2,1)} %wflux_ref.1, ...), custom_call_target="tpu_custom_call" | custom-call | tf_op jit(solution)/shard_map/coupled_step/pallas_call | solution.py:387
  48.8 2.3 %store_results.1 = (bf16[32,256,256]{2,1,0:T(8,128)(2,1)}, f32[80,8,256]{2,1,0:T(8,128)}, f32[32,256]{1,0:T(8,128)}) custom-call(bf16[32,256,256]{2,1,0:T(8,128)(2,1)S(1)} %get-tuple-element.9.state, f32[80,8,256]{2,1,0:T(8,128)S(1)} %get-tuple-element.10.following, f32[32,2,128]{2,1,0:T(2,128)S(1)} %get-tuple-element.11.temp), custom_call_target="tpu_custom_call" | custom-call | tf_op jit(solution)/shard_map/store_results/pallas_call | solution.py:356
